TPU v7x, 32 devices: a whole 2x2x4 slice. The times are simulated.
32 devices in a mesh: row: 4 (over z), col: 8 (over y, x, core).
Axes of the slice: x: 2, y: 2, z: 4, core: 2. Of those that a mesh axis runs over, the one named last changes fastest.
Arguments:
- covariance: float32 [16384, 16384], P('row', 'col'), as said below
- fields: float32 [512, 16384], P('col', 'row'), may hold values from -6 to 6
Outputs:
- factored: float32 [16384, 16384], P('row', 'col')
- solved_fields: float32 [512, 16384], P('col', 'row')
Inputs may be any that keep to these rules, and one draw needn't show every extreme that they name: covariance, read in the global order of the steps, is symmetric positive definite.
All inputs are finite; a program needn't handle non-finite values.
Results may differ from a plain program's by a relative error of at most 0.0003.
Values sent between devices are 32-bit elements; how exact they have to be, the bound alone decides.
A program may use at most 192 MiB of HBM per device.

v0:
```python
import jax
import jax.numpy as jnp
from jax import lax
from jax.sharding import PartitionSpec as P

NB = 512


PRECISE = lax.Precision.HIGHEST


def spread(block, axis, holder):
    block = jnp.where(lax.axis_index(axis) == holder, block, jnp.zeros_like(block))
    return lax.psum(block, axis)


def global_index(count, block, groups, index):
    local = jnp.arange(count, dtype=jnp.int32)
    return (local // block * groups + index) * block + local % block


def contract(left, right):
    return lax.dot_general(
        left, right, (((1,), (1,)), ((), ())), precision=PRECISE, preferred_element_type=jnp.float32
    )


def diagonal_block(matrix, field_local, step, block, ratio):
    row_count = lax.axis_size("row")
    stripe = ratio * block
    upper = step * stripe
    corner = matrix[upper : upper + stripe, step * block : (step + 1) * block]
    field_strip = field_local[:, upper : upper + stripe]
    width_fields = field_local.shape[0]
    across = lax.all_gather(corner, "col", axis=1, tiled=True)
    stacked, gathered = (
        lax.all_gather(across, "row", axis=0, tiled=True),
        lax.all_gather(field_strip, "row", axis=1, tiled=True),
    )
    square = stacked.reshape(row_count, ratio, block, NB).transpose(1, 0, 2, 3).reshape(NB, NB)
    gathered = (
        gathered.reshape(width_fields, row_count, ratio, block)
        .transpose(0, 2, 1, 3)
        .reshape(width_fields, NB)
    )
    factor = jnp.linalg.cholesky(square)
    inverse = jax.scipy.linalg.solve_triangular(factor, jnp.eye(NB, dtype=jnp.float32), lower=True)
    return (factor, inverse, gathered)


def factor_step(matrix, field_local, step, global_rows, block, ratio):
    row_count = lax.axis_size("row")
    row_index = lax.axis_index("row")
    column_index = lax.axis_index("col")
    local_rows = matrix.shape[0]
    width_fields = field_local.shape[0]
    stripe = ratio * block
    upper = step * stripe
    lower_bound = step * NB
    upper_bound = lower_bound + NB
    factor, inverse, gathered = diagonal_block(matrix, field_local, step, block, ratio)
    local_panel = matrix[:, step * block : (step + 1) * block]
    product = contract(lax.all_gather(local_panel, "col", axis=1, tiled=True), inverse)
    own_factor = lax.dynamic_index_in_dim(
        factor.reshape(ratio, row_count, block, NB), row_index, 1, keepdims=False
    )
    column = jnp.where(global_rows[:, None] < lower_bound, 0.0, product)
    column = column.at[upper : upper + stripe].set(own_factor.reshape(stripe, NB))
    trail = jnp.where(global_rows[:, None] >= upper_bound, column, 0.0)
    picked = lax.dynamic_index_in_dim(
        trail.reshape(local_rows // stripe, ratio, block, NB),
        column_index // row_count,
        1,
        keepdims=False,
    )
    transposed = spread(picked.reshape(local_rows // ratio, NB), "row", column_index % row_count)
    solved = contract(gathered, inverse)
    field_local = field_local - contract(solved, trail)
    own_solved = lax.dynamic_index_in_dim(
        solved.reshape(width_fields, ratio, row_count, block), row_index, 2, keepdims=False
    )
    field_local = field_local.at[:, upper : upper + stripe].set(
        own_solved.reshape(width_fields, stripe)
    )
    edge = lax.dynamic_slice_in_dim(column, column_index * block, block, 1)
    return (trail, transposed, field_local, edge)


def update(matrix, trail, transposed, first, last):
    return matrix.at[:, first:last].add(-contract(trail, transposed[first:last]))


def shards(covariance, fields):
    row_count = lax.axis_size("row")
    column_count = lax.axis_size("col")
    local_rows, local_columns = covariance.shape
    block = NB // column_count
    ratio = column_count // row_count
    global_rows = global_index(local_rows, block, row_count, lax.axis_index("row"))
    trail, transposed, field_local, edge_first = factor_step(
        covariance, fields, 0, global_rows, block, ratio
    )
    matrix = update(covariance, trail, transposed, block, local_columns)
    trail_next, transposed_next, field_local, edge_next = factor_step(
        matrix, field_local, 1, global_rows, block, ratio
    )
    matrix = update(matrix, trail_next, transposed_next, 2 * block, local_columns)
    remainder = jnp.where(global_rows[:, None] < 2 * NB, 0.0, matrix[:, 2 * block :])
    factored = jnp.concatenate([edge_first, edge_next, remainder], axis=1)
    return (factored, field_local)


def solution(mesh):
    return jax.shard_map(
        shards,
        mesh=mesh,
        in_specs=(P("row", "col"), P("col", "row")),
        out_specs=(P("row", "col"), P("col", "row")),
        check_vma=False,
    )
```

profile of v0, /device:TPU:0, one launch (start us, length us, event | category | flops | bytes accessed | tf_op | source)
XLA Modules:
  0.0 952.2 jit_solution(8926603900861421189)
XLA Ops:
  23.4 24.8 %all-gather.5.cloned.1.call-done = f32[512,512]{1,0:T(8,128)} async-done(((f32[128,512]{1,0:T(8,128)}), f32[512,512]{1,0:T(8,128)}) %all-gather.5.cloned.1.call-update) | async-done | bytes 1048592 | tf_op jit(solution)/shard_map/all_gather | solution.py:37
  51.1 11.7 %cholesky.286 = f32[128,128]{1,0:T(8,128)S(1)} custom-call(f32[128,128]{1,0:T(8,128)S(1)} %cholesky.426), custom_call_target="Cholesky" | custom-call | tf_op jit(solution)/shard_map/jit(cholesky)/cholesky | solution.py:46
  75.3 11.7 %cholesky.305 = f32[128,128]{1,0:T(8,128)S(1)} custom-call(f32[128,128]{1,0:T(8,128)S(1)} %cholesky.430), custom_call_target="Cholesky" | custom-call | tf_op jit(solution)/shard_map/jit(cholesky)/cholesky | solution.py:46
  98.7 11.7 %cholesky.326 = f32[128,128]{1,0:T(8,128)S(1)} custom-call(f32[128,128]{1,0:T(8,128)S(1)} %cholesky.435), custom_call_target="Cholesky" | custom-call | tf_op jit(solution)/shard_map/jit(cholesky)/cholesky | solution.py:46
  121.7 11.7 %cholesky.343 = f32[128,128]{1,0:T(8,128)S(1)} custom-call(f32[128,128]{1,0:T(8,128)S(1)} %convolution_subtract_fusion.13), custom_call_target="Cholesky" | custom-call | tf_op jit(solution)/shard_map/jit(cholesky)/cholesky | solution.py:46
  146.3 39.3 %custom-call.30 = f32[4,128,128]{1,2,0:T(8,128)S(1)} custom-call(f32[4,128,128]{2,1,0:T(8,128)S(1)} %get-tuple-element.90), custom_call_target="InvertDiagBlocksLowerTriangular" | custom-call | tf_op jit(solution)/shard_map/jit(_solve_triangular)/triangular_solve | solution.py:47
  190.6 16.5 %select_bitcast_fusion = f32[4096,512]{0,1:T(8,128)S(1)} fusion(f32[4096,512]{0,1:T(8,128)} %all-gather.7.cloned.1.call-done, pred[4096]{0:T(1024)(128)(4,1)S(1)} %get-tuple-element.149, f32[128,512]{1,0:T(8,128)S(1)} %fusion.53, f32[128,512]{1,0:T(8,128)S(1)} %fusion.54, f32[128,512]{1,0:T(8,128)S(1)} %fusion.56, f32[128,512]{1,0:T(8,128)S(1)} %fusion.31), kind=kOutput, calls=%fused_computation.8 | convolution fusion | flops 12887785472 | bytes 17829888 | tf_op jit(solution)/shard_map/dot_general | solution.py:23
  228.6 25.5 %slice.220 = f32[4096,1984]{1,0:T(8,128)} slice(f32[4096,2048]{1,0:T(8,128)} %param.17), slice={[0:4096], [64:2048]} | slice | bytes 65011712 | tf_op jit(solution)/shard_map/slice.186
  254.1 30.9 %copy.71 = f32[4096,1984]{0,1:T(8,128)} copy(f32[4096,1984]{1,0:T(8,128)} %slice.220) | data formatting | bytes 65011712
  285.0 98.1 %all-reduce.4.cloned.1.call-done = f32[2048,512]{1,0:T(8,128)} async-done(((f32[2048,512]{1,0:T(8,128)}), f32[2048,512]{1,0:T(8,128)}) %all-reduce.4.cloned.1.call-update) | async-done | bytes 4194320 | tf_op jit(solution)/shard_map/psum | solution.py:14
  383.2 59.1 %negate_add_fusion = f32[4096,1984]{0,1:T(8,128)} fusion(f32[4096,1984]{0,1:T(8,128)} %copy.71, f32[4096,512]{0,1:T(8,128)} %broadcast_select_fusion.1, f32[2048,512]{1,0:T(8,128)} %all-reduce.4.cloned.1.call-done), kind=kOutput, calls=%fused_computation.5 | convolution fusion | flops 49945247744 | bytes 77463552 | tf_op jit(solution)/shard_map/dot_general | solution.py:23
  456.2 25.6 %all-gather.11.cloned.1.call-done = f32[512,512]{0,1:T(8,128)} async-done(((f32[128,512]{0,1:T(8,128)}), f32[512,512]{0,1:T(8,128)}) %all-gather.11.cloned.1.call-update) | async-done | bytes 1048592 | tf_op jit(solution)/shard_map/all_gather | solution.py:37
  489.5 11.7 %cholesky.358 = f32[128,128]{1,0:T(8,128)S(1)} custom-call(f32[128,128]{1,0:T(8,128)S(1)} %cholesky.439), custom_call_target="Cholesky" | custom-call | tf_op jit(solution)/shard_map/jit(cholesky)/cholesky | solution.py:46
  513.8 11.7 %cholesky.377 = f32[128,128]{1,0:T(8,128)S(1)} custom-call(f32[128,128]{1,0:T(8,128)S(1)} %cholesky.443), custom_call_target="Cholesky" | custom-call | tf_op jit(solution)/shard_map/jit(cholesky)/cholesky | solution.py:46
  537.1 11.7 %cholesky.398 = f32[128,128]{1,0:T(8,128)S(1)} custom-call(f32[128,128]{1,0:T(8,128)S(1)} %cholesky.448), custom_call_target="Cholesky" | custom-call | tf_op jit(solution)/shard_map/jit(cholesky)/cholesky | solution.py:46
  560.1 11.9 %cholesky.415 = f32[128,128]{1,0:T(8,128)S(1)} custom-call(f32[128,128]{1,0:T(8,128)S(1)} %convolution_subtract_fusion.12), custom_call_target="Cholesky" | custom-call | tf_op jit(solution)/shard_map/jit(cholesky)/cholesky | solution.py:46
  589.9 39.3 %custom-call.34 = f32[4,128,128]{1,2,0:T(8,128)S(1)} custom-call(f32[4,128,128]{2,1,0:T(8,128)S(1)} %get-tuple-element.91), custom_call_target="InvertDiagBlocksLowerTriangular" | custom-call | tf_op jit(solution)/shard_map/jit(_solve_triangular)/triangular_solve | solution.py:47
  635.9 17.6 %convolution_select_fusion = f32[4096,512]{0,1:T(8,128)S(1)} fusion(f32[4096,512]{0,1:T(8,128)} %all-gather.9.cloned.1.call-done, pred[4096]{0:T(1024)(128)(4,1)S(1)} %broadcast_compare_fusion.3, f32[128,512]{1,0:T(8,128)S(1)} %fusion.47, f32[128,512]{1,0:T(8,128)S(1)} %fusion.48, f32[128,512]{1,0:T(8,128)S(1)} %fusion.50, f32[128,512]{1,0:T(8,128)S(1)} %fusion.29), kind=kOutput, calls=%fused_computation.9 | convolution fusion | flops 12887785472 | bytes 17829888 | tf_op jit(solution)/shard_map/dot_general | solution.py:23
  674.7 14.7 %all_gather.30 = f32[64,512]{1,0:T(8,128)S(1)} all-gather(f32[64,128]{1,0:T(8,128)S(1)} %slice-done), channel_id=1, replica_groups=mesh['row'=4,'col'=8] {'row'}, dimensions={1}, use_global_device_ids=true | all-gather | bytes 163840 | tf_op jit(solution)/shard_map/all_gather | solution.py:38
  701.5 15.7 %all_gather.31 = f32[64,512]{1,0:T(8,128)S(1)} all-gather(f32[64,128]{1,0:T(8,128)S(1)} %slice.249), channel_id=1, replica_groups=mesh['row'=4,'col'=8] {'row'}, dimensions={1}, use_global_device_ids=true | all-gather | bytes 163840 | tf_op jit(solution)/shard_map/all_gather | solution.py:38
  730.4 100.8 %all-reduce.6.cloned.1.call-done = f32[2048,512]{1,0:T(8,128)} async-done(((f32[2048,512]{1,0:T(8,128)}), f32[2048,512]{1,0:T(8,128)}) %all-reduce.6.cloned.1.call-update) | async-done | bytes 4194320 | tf_op jit(solution)/shard_map/psum | solution.py:14
  831.2 58.4 %fusion = f32[4096,1920]{0,1:T(8,128)} fusion(f32[4096,1984]{0,1:T(8,128)} %negate_add_fusion, f32[4096,512]{0,1:T(8,128)} %broadcast_select_fusion, pred[4096]{0:T(1024)(128)(4,1)S(1)} %broadcast_compare_fusion.1, f32[2048,512]{1,0:T(8,128)} %all-reduce.6.cloned.1.call-done), kind=kOutput, calls=%fused_computation.7 | convolution fusion | flops 48341975040 | bytes 75239424 | tf_op jit(solution)/shard_map/dot_general | solution.py:23
  889.6 22.2 %pad_maximum_fusion = f32[4096,2048]{0,1:T(8,128)} fusion(f32[4096,1920]{0,1:T(8,128)} %fusion, f32[4096,64]{0,1:T(8,128)S(1)} %constant_dynamic-slice_fusion.3, f32[4096,64]{0,1:T(8,128)S(1)} %constant_dynamic-slice_fusion.5), kind=kLoop, calls=%fused_computation.4 | loop fusion | flops 16777216 | bytes 67108864 | tf_op jit(solution)/shard_map/concatenate | solution.py:109
  911.8 33.3 %copy.66 = f32[4096,2048]{1,0:T(8,128)} copy(f32[4096,2048]{0,1:T(8,128)} %pad_maximum_fusion) | data formatting | bytes 67108864
  (181 shorter events, 235.2 us)
Async XLA Ops:
  7.2 41.0 %all-gather.5.cloned.1.call-start = ((), (), s32[]{:S(2)}) async-start(), calls=%async_computation | async-start | bytes 1310720 | tf_op jit(solution)/shard_map/all_gather | solution.py:37
  19.8 170.9 %all-gather.7.cloned.1.call-start = ((), (), s32[]{:S(2)}) async-start(), calls=%async_computation.1 | async-start | bytes 9437184 | tf_op jit(solution)/shard_map/all_gather | solution.py:63
  23.1 360.0 %all-reduce.4.cloned.1.call-start = ((), (), s32[]{:S(2)}) async-start(), calls=%async_computation.2 | async-start | bytes 8388608 | tf_op jit(solution)/shard_map/psum | solution.py:14
  50.1 1.0 copy-start.3
  146.3 39.8 %copy-start.2 = (f32[512,512]{1,0:T(8,128)}, f32[512,512]{1,0:T(8,128)S(1)}, u32[]{:S(2)}) copy-start(f32[512,512]{1,0:T(8,128)S(1)} %get-tuple-element.259) | copy-start | bytes 3145732
  190.6 16.6 %copy-start.6 = (f32[128,512]{1,0:T(8,128)}, f32[128,512]{1,0:T(8,128)S(1)}, u32[]{:S(2)}) copy-start(f32[128,512]{1,0:T(8,128)S(1)} %fusion.53) | copy-start | bytes 786436
  207.2 3.2 copy-start.1
  228.5 253.3 %all-gather.11.cloned.1.call-start = ((), (), s32[]{:S(2)}) async-start(), calls=%async_computation.4 | async-start | bytes 1310720 | tf_op jit(solution)/shard_map/all_gather | solution.py:37
  453.4 182.6 %all-gather.9.cloned.1.call-start = ((), (), s32[]{:S(2)}) async-start(), calls=%async_computation.3 | async-start | bytes 9437184 | tf_op jit(solution)/shard_map/all_gather | solution.py:63
  455.7 375.5 %all-reduce.6.cloned.1.call-start = ((), (), s32[]{:S(2)}) async-start(), calls=%async_computation.5 | async-start | bytes 8388608 | tf_op jit(solution)/shard_map/psum | solution.py:14
  488.5 1.1 copy-start.4
  629.2 3.4 copy-start.10
  635.9 17.6 %copy-start.8 = (f32[128,512]{1,0:T(8,128)}, f32[128,512]{1,0:T(8,128)S(1)}, u32[]{:S(2)}) copy-start(f32[128,512]{1,0:T(8,128)S(1)} %fusion.47) | copy-start | bytes 786436
  653.6 3.2 copy-start
  669.7 5.0 slice-start
  669.7 21.6 %copy-start.7 = (f32[128,512]{1,0:T(8,128)S(1)}, f32[128,512]{1,0:T(8,128)}, u32[]{:S(2)}) copy-start(f32[128,512]{1,0:T(8,128)} %copy-done.6) | copy-start | bytes 786436
  692.4 26.5 %copy-start.9 = (f32[128,512]{1,0:T(8,128)S(1)}, f32[128,512]{1,0:T(8,128)}, u32[]{:S(2)}) copy-start(f32[128,512]{1,0:T(8,128)} %copy-done.8) | copy-start | bytes 786436
  728.7 160.9 %copy-start.5 = (f32[64,4096]{1,0:T(8,128)}, f32[64,4096]{1,0:T(8,128)S(1)}, u32[]{:S(2)}) copy-start(f32[64,4096]{1,0:T(8,128)S(1)} %fusion.65) | copy-start | bytes 3145732
Sparse Core Ops, SparseCore 0:
  19.9 28.2 all-gather.4
  50.6 53.9 all-gather.6
  228.7 154.4 all-reduce.3
  453.5 28.2 all-gather.10
  484.3 52.9 all-gather.8
  674.8 156.3 all-reduce.5
where the time goes:
time: 965 us; the launch traced here: 952 us
  other arithmetic  283 us (29%)
  waiting for transfers between devices  249 us (26%)
  matrix products  192 us (20%)
  local copies, waits for them, and re-layouts  156 us (16%)
  blocking collectives  51.5 us (5%)
  between operations  20.1 us (2%)
    psum x2, waiting for transfers between devices, spread(): return lax.psum(block, axis)  199 us
    dot_general x8, matrix products, contract(): lax.dot_general(left, right, (((1,), (1,)), ((), ())), precision=PRECISE,...  169 us
    another operation x29, other arithmetic, diagonal_block(): factor = jnp.linalg.cholesky(square)  158 us
    another operation x5, other arithmetic, diagonal_block(): jax.scipy.linalg.solve_triangular(factor, jnp.eye(NB, dtype=jnp.float32),...  80.2 us
    unnamed x26, local copies, waits for them, and re-layouts  74.4 us
    all_gather x2, waiting for transfers between devices, diagonal_block(): lax.all_gather(across, 'row', axis=0, tiled=True)  50.4 us
    all_gather x2, blocking collectives, diagonal_block(): lax.all_gather(field_strip, 'row', axis=1, tiled=True)  30.4 us
    another operation x5, local copies, waits for them, and re-layouts  26 us
  transfers between devices with their start and end apart: 6, of which 4 were waited for; matrix products, arithmetic and copies ran while one was open for 40% of the time, Pallas kernels for 0%

commit v1 on v0

v1 whole, which is shorter than its diff:
```python
import functools

import jax
import jax.numpy as jnp
from jax import lax
from jax.experimental import pallas as pl
from jax.experimental.pallas import tpu as pltpu
from jax.sharding import PartitionSpec as P

NB = 512

EXACT = lax.Precision.HIGHEST
PANEL = lax.Precision.HIGH


def dot(left, right, left_axis, right_axis, precision):
    return lax.dot_general(
        left,
        right,
        (((left_axis,), (right_axis,)), ((), ())),
        precision=precision,
        preferred_element_type=jnp.float32,
    )


def split(value):
    high = value.astype(jnp.bfloat16)
    return high, (value - high.astype(jnp.float32)).astype(jnp.bfloat16)


def update_kernel(top, width, chunk, a_ref, p0_ref, p1_ref, q0_ref, q1_ref, edge_ref, o_ref, high, low):
    tile, columns = a_ref.shape
    step = pl.program_id(0)

    @pl.when(step == 0)
    def _():
        for k, ref in enumerate((q0_ref, q1_ref)):
            for at in range(0, NB, 64):
                upper, lower = split(ref[at : at + 64, :])
                high[k * NB + at : k * NB + at + 64, :] = upper
                low[k * NB + at : k * NB + at + 64, :] = lower

    p_high, p_low = split(jnp.concatenate([p0_ref[...], p1_ref[...]], axis=1))
    rows = step * tile + lax.broadcasted_iota(jnp.int32, (tile, chunk), 0)
    for at in range(0, columns, chunk):
        here = slice(at, at + chunk)
        right_high = high[:, here]
        total = jnp.dot(p_high, right_high, preferred_element_type=jnp.float32)
        total += jnp.dot(p_low, right_high, preferred_element_type=jnp.float32)
        total += jnp.dot(p_high, low[:, here], preferred_element_type=jnp.float32)
        o_ref[:, here] = jnp.where(rows < top, 0.0, a_ref[:, here] - total)
    o_ref[:, :width] = edge_ref[...]


def update(matrix, p0, p1, q0, q1, edge, top):
    rows, columns = matrix.shape
    tile = min(256, rows)
    chunk = min(512, columns)
    width = edge.shape[1]
    return pl.pallas_call(
        functools.partial(update_kernel, top, width, chunk),
        grid=(rows // tile,),
        out_shape=jax.ShapeDtypeStruct(matrix.shape, jnp.float32),
        in_specs=[
            pl.BlockSpec((tile, columns), lambda i: (i, 0)),
            pl.BlockSpec((tile, NB), lambda i: (i, 0)),
            pl.BlockSpec((tile, NB), lambda i: (i, 0)),
            pl.BlockSpec((NB, columns), lambda i: (0, 0)),
            pl.BlockSpec((NB, columns), lambda i: (0, 0)),
            pl.BlockSpec((tile, width), lambda i: (i, 0)),
        ],
        out_specs=pl.BlockSpec((tile, columns), lambda i: (i, 0)),
        scratch_shapes=[
            pltpu.VMEM((2 * NB, columns), jnp.bfloat16),
            pltpu.VMEM((2 * NB, columns), jnp.bfloat16),
        ],
        compiler_params=pltpu.CompilerParams(vmem_limit_bytes=56 * 1024 * 1024),
        cost_estimate=pl.CostEstimate(
            flops=12 * NB * rows * columns, bytes_accessed=8 * rows * columns, transcendentals=0
        ),
    )(matrix, p0, p1, q0, q1, edge)


def factor_block(square):
    factor = jnp.linalg.cholesky(square)
    inverse = jax.scipy.linalg.solve_triangular(factor, jnp.eye(NB, dtype=jnp.float32), lower=True)
    return factor, inverse


def shards(covariance, fields):
    row_count = lax.axis_size("row")
    column_count = lax.axis_size("col")
    row_index = lax.axis_index("row")
    column_index = lax.axis_index("col")
    local_rows, local_columns = covariance.shape
    width_fields = fields.shape[0]
    block = NB // column_count
    ratio = column_count // row_count
    stripe = ratio * block

    def order_rows(stacked, steps):
        tail = stacked.shape[1]
        stacked = stacked.reshape(row_count, steps * ratio, block, tail)
        return stacked.transpose(1, 0, 2, 3).reshape(steps * NB, tail)

    def own_rows(value):
        return own_rows_of(value, ratio, row_count, block, row_index)

    def corner(piece, steps):
        across = lax.all_gather(piece, "col", axis=1, tiled=True)
        return order_rows(lax.all_gather(across, "row", axis=0, tiled=True), steps)

    first = corner(covariance[:stripe, :block], 1)
    second = corner(covariance[: 2 * stripe, block : 2 * block], 2)
    panel = lax.all_gather(covariance[:, : 2 * block].T, "col", axis=0, tiled=True)
    panel = panel.reshape(column_count, 2, block, local_rows).transpose(1, 0, 2, 3)
    panel = panel.reshape(2, NB, local_rows)
    across = order_rows(lax.all_gather(covariance[: 2 * stripe], "row", axis=0, tiled=True), 2)
    strip = order_rows(lax.all_gather(fields[:, : 2 * stripe].T, "row", axis=0, tiled=True), 2)

    factor0, inverse0 = factor_block(first)
    side = dot(inverse0, second[:NB], 1, 0, EXACT)
    factor1, inverse1 = factor_block(second[NB:] - dot(side, side, 0, 0, EXACT))

    p0 = dot(panel[0], inverse0, 0, 1, PANEL)
    p1 = dot(panel[1].T - dot(p0, side, 1, 0, PANEL), inverse1, 1, 1, PANEL)
    q0 = dot(inverse0, across[:NB], 1, 0, PANEL)
    q1 = dot(inverse1, across[NB:] - dot(side, q0, 0, 0, PANEL), 1, 0, PANEL)
    y0 = dot(inverse0, strip[:NB], 1, 0, EXACT)
    y1 = dot(inverse1, strip[NB:] - dot(side, y0, 0, 0, EXACT), 1, 0, EXACT)

    start = column_index * block
    edge0 = lax.dynamic_slice_in_dim(p0, start, block, 1)
    edge1 = lax.dynamic_slice_in_dim(p1, start, block, 1)
    own0 = lax.dynamic_slice_in_dim(own_rows(factor0), start, block, 1)
    own1 = lax.dynamic_slice_in_dim(own_rows(factor1), start, block, 1)
    edge0 = jnp.concatenate([own0, edge0[stripe:]], axis=0)
    edge1 = jnp.concatenate([jnp.zeros_like(own1), own1, edge1[2 * stripe :]], axis=0)
    edge = jnp.concatenate([edge0, edge1], axis=1)
    factored = update(covariance, p0, p1, q0, q1, edge, 2 * stripe)

    moved = fields - dot(y0, p0, 0, 1, PANEL) - dot(y1, p1, 0, 1, PANEL)
    head = [own_rows(y0), own_rows(y1)]
    solved = jnp.concatenate([head[0].T, head[1].T, moved[:, 2 * stripe :]], axis=1)
    return (factored, solved)


def own_rows_of(value, ratio, row_count, block, row_index):
    tail = value.shape[1]
    picked = lax.dynamic_index_in_dim(
        value.reshape(ratio, row_count, block, tail), row_index, 1, keepdims=False
    )
    return picked.reshape(ratio * block, tail)


def solution(mesh):
    return jax.shard_map(
        shards,
        mesh=mesh,
        in_specs=(P("row", "col"), P("col", "row")),
        out_specs=(P("row", "col"), P("col", "row")),
        check_vma=False,
    )
```

time: 965 us -> 564 us (0.58)
  waiting for transfers between devices: 249 us -> 0.11 us
  matrix products: 192 us -> 84.2 us
  Pallas kernels: 0 us -> 63.3 us
  local copies, waits for them, and re-layouts: 156 us -> 105 us
  other arithmetic: 283 us -> 250 us
  blocking collectives: 51.5 us -> 36.5 us
    psum x2 -> x0, waiting for transfers between devices: 199 us -> none  [spread(): return lax.psum(block, axis)]
    dot_general x8 -> x13, matrix products: 169 us -> 56.7 us  [dot(): lax.dot_general(left, right, (((left_axis,), (right_axis,)), ((), ())), p...]
    unnamed x26 -> x33, local copies, waits for them, and re-layouts: 74.4 us -> 8.24 us
    pallas_call x0 -> x1, Pallas kernels: none -> 63.3 us  [update(): pl.pallas_call(functools.partial(update_kernel, top, width, chunk), grid=...]
    all_gather x4, waiting for transfers between devices: 50.5 us -> 0.04 us  [the longest x2 0.02 us: corner(): return order_rows(lax.all_gather(across, 'row', axis=0, tiled=True), steps)]
    slice x7 -> x18, local copies, waits for them, and re-layouts: 5.62 us -> 30.1 us  [the longest x1 10.1 us: shards(): p1 = dot(panel[1].T - dot(p0, side, 1, 0, PANEL), inverse1, 1, 1, PANEL)]
    another operation x40 -> x35, local copies, waits for them, and re-layouts: 45.3 us -> 24.3 us  [the longest x27 23.1 us: factor_block(): jax.scipy.linalg.solve_triangular(factor, jnp.eye(NB, dtype=jnp.float32),...]
    concatenate x1 -> x2, other arithmetic: 22.2 us -> 3 us  [the longest x1 1.96 us: shards(): edge = jnp.concatenate([edge0, edge1], axis=1)]
  transfers between devices with their start and end apart: 6 -> 4, of which waited for: 4 -> 0; matrix products, arithmetic and copies ran while one was open for 40% -> 62% of each run, Pallas kernels for 0% -> 0%
where the time goes in v1:
time: 564 us; the launch traced here: 559 us
  other arithmetic  250 us (44%)
  local copies, waits for them, and re-layouts  105 us (19%)
  matrix products  84.2 us (15%)
  Pallas kernels  63.3 us (11%)
  blocking collectives  36.5 us (6%)
  between operations  19.8 us (4%)
    another operation x29, other arithmetic, factor_block(): factor = jnp.linalg.cholesky(square)  160 us
    another operation x5, other arithmetic, factor_block(): jax.scipy.linalg.solve_triangular(factor, jnp.eye(NB, dtype=jnp.float32),...  83.2 us
    pallas_call x1, Pallas kernels, update(): pl.pallas_call(functools.partial(update_kernel, top, width, chunk), grid=...  63.3 us
    dot_general x13, matrix products, dot(): lax.dot_general(left, right, (((left_axis,), (right_axis,)), ((), ())), p...  56.7 us
    another operation x27, local copies, waits for them, and re-layouts, factor_block(): jax.scipy.linalg.solve_triangular(factor, jnp.eye(NB, dtype=jnp.float32),...  23.1 us
    all_gather x2, blocking collectives, corner(): across = lax.all_gather(piece, 'col', axis=1, tiled=True)  20.6 us
    dot_general x2, local copies, waits for them, and re-layouts, dot(): lax.dot_general(left, right, (((left_axis,), (right_axis,)), ((), ())), p...  18.2 us
    all_gather x1, blocking collectives, shards(): lax.all_gather(fields[:, :2 * stripe].T, 'row', axis=0, tiled=True)  15.9 us
  transfers between devices with their start and end apart: 4, of which 0 were waited for; matrix products, arithmetic and copies ran while one was open for 62% of the time, Pallas kernels for 0%

profile of v1, /device:TPU:0, one launch (start us, length us, event | category | flops | bytes accessed | tf_op | source)
XLA Modules:
  0.0 559.0 jit_solution(14167296431800962740)
XLA Ops:
  8.1 10.8 %all_gather.21 = f32[128,512]{0,1:T(8,128)S(1)} all-gather(f32[128,64]{0,1:T(8,128)S(1)} %copy.68), channel_id=1, replica_groups=mesh['row'=4,'col'=8] {'col'}, dimensions={1}, use_global_device_ids=true | all-gather | bytes 294912 | tf_op jit(solution)/shard_map/all_gather | solution.py:110
  20.9 9.8 %all_gather.24 = f32[256,512]{0,1:T(8,128)S(1)} all-gather(f32[256,64]{0,1:T(8,128)S(1)} %copy.70), channel_id=1, replica_groups=mesh['row'=4,'col'=8] {'col'}, dimensions={1}, use_global_device_ids=true | all-gather | bytes 589824 | tf_op jit(solution)/shard_map/all_gather | solution.py:110
  39.3 15.9 %all_gather.27 = f32[1024,64]{0,1:T(8,128)S(1)} all-gather(f32[256,64]{0,1:T(8,128)S(1)} %slice_bitcast_fusion.16), channel_id=1, replica_groups=mesh['row'=4,'col'=8] {'row'}, dimensions={0}, use_global_device_ids=true | all-gather | bytes 327680 | tf_op jit(solution)/shard_map/all_gather | solution.py:119
  61.9 11.7 %cholesky.286 = f32[128,128]{1,0:T(8,128)S(1)} custom-call(f32[128,128]{1,0:T(8,128)S(1)} %cholesky.426), custom_call_target="Cholesky" | custom-call | tf_op jit(solution)/shard_map/jit(cholesky)/cholesky | solution.py:85
  73.6 9.8 %custom-call.27 = f32[1,128,128]{1,2,0:T(8,128)S(1)} custom-call(f32[1,128,128]{2,1,0:T(8,128)S(1)} %get-tuple-element.71), custom_call_target="InvertDiagBlocksLowerTriangular" | custom-call | tf_op jit(solution)/shard_map/jit(cholesky)/cholesky | solution.py:85
  86.1 11.7 %cholesky.305 = f32[128,128]{1,0:T(8,128)S(1)} custom-call(f32[128,128]{1,0:T(8,128)S(1)} %cholesky.430), custom_call_target="Cholesky" | custom-call | tf_op jit(solution)/shard_map/jit(cholesky)/cholesky | solution.py:85
  98.2 9.8 %custom-call.28 = f32[1,128,128]{1,2,0:T(8,128)S(1)} custom-call(f32[1,128,128]{2,1,0:T(8,128)S(1)} %get-tuple-element.68), custom_call_target="InvertDiagBlocksLowerTriangular" | custom-call | tf_op jit(solution)/shard_map/jit(cholesky)/cholesky | solution.py:85
  109.6 11.7 %cholesky.326 = f32[128,128]{1,0:T(8,128)S(1)} custom-call(f32[128,128]{1,0:T(8,128)S(1)} %cholesky.435), custom_call_target="Cholesky" | custom-call | tf_op jit(solution)/shard_map/jit(cholesky)/cholesky | solution.py:85
  121.4 9.8 %custom-call.29 = f32[1,128,128]{1,2,0:T(8,128)S(1)} custom-call(f32[1,128,128]{2,1,0:T(8,128)S(1)} %get-tuple-element.65), custom_call_target="InvertDiagBlocksLowerTriangular" | custom-call | tf_op jit(solution)/shard_map/jit(cholesky)/cholesky | solution.py:85
  132.6 11.9 %cholesky.343 = f32[128,128]{1,0:T(8,128)S(1)} custom-call(f32[128,128]{1,0:T(8,128)S(1)} %convolution_subtract_fusion.13), custom_call_target="Cholesky" | custom-call | tf_op jit(solution)/shard_map/jit(cholesky)/cholesky | solution.py:85
  150.7 11.6 %while.4 = (s32[]{:T(128)}, f32[512,512]{1,0:T(8,128)}, s32[4,2]{0,1:T(2,128)S(1)}, f32[4,128,128]{2,1,0:T(8,128)S(1)}, s32[]{:T(128)}) while((s32[]{:T(128)}, f32[512,512]{1,0:T(8,128)}, s32[4,2]{0,1:T(2,128)S(1)}, f32[4,128,128]{2,1,0:T(8,128)S(1)}, s32[]{:T(128)}) %tuple.61), condition=%wide.while_cond, body=%wide.while_body.sunk | while | flops 2 | bytes 131189 | solution.py:86
  162.3 39.3 %custom-call.30 = f32[4,128,128]{1,2,0:T(8,128)S(1)} custom-call(f32[4,128,128]{2,1,0:T(8,128)S(1)} %get-tuple-element.18), custom_call_target="InvertDiagBlocksLowerTriangular" | custom-call | tf_op jit(solution)/shard_map/jit(_solve_triangular)/triangular_solve | solution.py:86
  227.0 12.1 %cholesky.358 = f32[128,128]{1,0:T(8,128)S(1)} custom-call(f32[128,128]{1,0:T(8,128)S(1)} %cholesky.439), custom_call_target="Cholesky" | custom-call | tf_op jit(solution)/shard_map/jit(cholesky)/cholesky | solution.py:85
  239.1 9.8 %custom-call.31 = f32[1,128,128]{1,2,0:T(8,128)S(1)} custom-call(f32[1,128,128]{2,1,0:T(8,128)S(1)} %get-tuple-element.61), custom_call_target="InvertDiagBlocksLowerTriangular" | custom-call | tf_op jit(solution)/shard_map/jit(cholesky)/cholesky | solution.py:85
  253.2 11.7 %cholesky.377 = f32[128,128]{1,0:T(8,128)S(1)} custom-call(f32[128,128]{1,0:T(8,128)S(1)} %cholesky.443), custom_call_target="Cholesky" | custom-call | tf_op jit(solution)/shard_map/jit(cholesky)/cholesky | solution.py:85
  265.5 9.8 %custom-call.32 = f32[1,128,128]{1,2,0:T(8,128)S(1)} custom-call(f32[1,128,128]{2,1,0:T(8,128)S(1)} %get-tuple-element.58), custom_call_target="InvertDiagBlocksLowerTriangular" | custom-call | tf_op jit(solution)/shard_map/jit(cholesky)/cholesky | solution.py:85
  277.7 11.9 %cholesky.398 = f32[128,128]{1,0:T(8,128)S(1)} custom-call(f32[128,128]{1,0:T(8,128)S(1)} %cholesky.448), custom_call_target="Cholesky" | custom-call | tf_op jit(solution)/shard_map/jit(cholesky)/cholesky | solution.py:85
  290.2 9.8 %custom-call.33 = f32[1,128,128]{1,2,0:T(8,128)S(1)} custom-call(f32[1,128,128]{2,1,0:T(8,128)S(1)} %get-tuple-element.55), custom_call_target="InvertDiagBlocksLowerTriangular" | custom-call | tf_op jit(solution)/shard_map/jit(cholesky)/cholesky | solution.py:85
  302.3 11.7 %cholesky.415 = f32[128,128]{1,0:T(8,128)S(1)} custom-call(f32[128,128]{1,0:T(8,128)S(1)} %convolution_subtract_fusion.12), custom_call_target="Cholesky" | custom-call | tf_op jit(solution)/shard_map/jit(cholesky)/cholesky | solution.py:85
  322.7 11.6 %while.5 = (s32[]{:T(128)}, f32[512,512]{1,0:T(8,128)}, s32[4,2]{0,1:T(2,128)S(1)}, f32[4,128,128]{2,1,0:T(8,128)S(1)}, s32[]{:T(128)}) while((s32[]{:T(128)}, f32[512,512]{1,0:T(8,128)}, s32[4,2]{0,1:T(2,128)S(1)}, f32[4,128,128]{2,1,0:T(8,128)S(1)}, s32[]{:T(128)}) %tuple.75), condition=%wide.while_cond.clone, body=%wide.while_body.clone.sunk | while | flops 2 | bytes 131189 | solution.py:86
  334.3 39.5 %custom-call.34 = f32[4,128,128]{1,2,0:T(8,128)S(1)} custom-call(f32[4,128,128]{2,1,0:T(8,128)S(1)} %get-tuple-element.19), custom_call_target="InvertDiagBlocksLowerTriangular" | custom-call | tf_op jit(solution)/shard_map/jit(_solve_triangular)/triangular_solve | solution.py:86
  405.0 10.1 %fusion.77 = (f32[1,8,64,4096]{3,2,0,1:T(8,128)}, f32[1,8,64,4096]{3,2,0,1:T(8,128)S(1)}) fusion(f32[2,8,64,4096]{3,2,0,1:T(8,128)} %bitcast.173), kind=kLoop, calls=%fused_computation.161 | loop fusion | bytes 33554432 | tf_op jit(solution)/shard_map/slice | solution.py:126
  454.5 10.7 %fusion = f32[4096,512]{0,1:T(8,128)S(1)} fusion(f32[4096,512]{1,0:T(8,128)} %fusion.81, f32[512,4096]{0,1:T(8,128)} %copy.51, f32[128,512]{1,0:T(8,128)S(1)} %fusion.45, f32[128,512]{1,0:T(8,128)S(1)} %copy-done.6, f32[128,512]{1,0:T(8,128)S(1)} %fusion.48, f32[128,512]{1,0:T(8,128)S(1)} %fusion.25), kind=kOutput, calls=%fused_computation.5 | convolution fusion | flops 6445334528 | bytes 26214400 | tf_op jit(solution)/shard_map/dot_general | solution.py:17
  489.0 63.3 %shard_map.41 = f32[4096,2048]{1,0:T(8,128)} custom-call(f32[4096,2048]{1,0:T(8,128)} %a_ref.1, f32[4096,512]{1,0:T(8,128)} %bitcast.175, f32[4096,512]{1,0:T(8,128)} %copy.65.p1_ref, f32[512,2048]{1,0:T(8,128)} %copy-done.2, f32[512,2048]{1,0:T(8,128)} %fusion.38.q1_ref, f32[4096,128]{1,0:T(8,128)} %maximum_maximum_fusion.edge_ref), custom_call_target="tpu_custom_call" | custom-call | flops 51539607552 | bytes 67108864 | tf_op jit(solution)/shard_map/pallas_call | solution.py:60
  (182 shorter events, 186.4 us)
Async XLA Ops:
  7.2 49.7 %all-gather.5.cloned.1.call-start = ((), (), s32[]{:S(2)}) async-start(), calls=%async_computation | async-start | bytes 1310720 | tf_op jit(solution)/shard_map/all_gather | solution.py:111
  19.8 191.6 %all-gather.9.cloned.1.call-start = ((), (), s32[]{:S(2)}) async-start(), calls=%async_computation.2 | async-start | bytes 2621440 | tf_op jit(solution)/shard_map/all_gather | solution.py:111
  31.7 355.2 %all-gather.11.cloned.1.call-start = ((), (), s32[]{:S(2)}) async-start(), calls=%async_computation.3 | async-start | bytes 10485760 | tf_op jit(solution)/shard_map/all_gather | solution.py:118
  35.0 1.6 slice-start
  35.0 370.0 %all-gather.7.cloned.1.call-start = ((), (), s32[]{:S(2)}) async-start(), calls=%async_computation.1 | async-start | bytes 18874368 | tf_op jit(solution)/shard_map/all_gather | solution.py:115
  60.9 1.0 copy-start.9
  207.5 9.4 %copy-start.3 = (f32[128,512]{1,0:T(8,128)}, f32[128,512]{1,0:T(8,128)S(1)}, u32[]{:S(2)}) copy-start(f32[128,512]{1,0:T(8,128)S(1)} %fusion.51) | copy-start | bytes 786436
  215.5 3.3 copy-start.7
  226.0 1.0 copy-start.10
  373.8 0.7 copy-start.13
  379.6 4.6 copy-start.5
  391.3 1.0 copy-start.4
  395.8 4.1 copy-start.2
  395.8 4.1 copy-start.6
  422.7 4.3 copy-start
  465.2 3.4 copy-start.1
  481.0 2.5 copy-start.8
  481.1 2.5 copy-start.11
  483.6 2.4 copy-start.14
  483.6 3.4 copy-start.12
Sparse Core Ops, SparseCore 0:
  19.9 31.0 all-gather.4
  52.5 45.4 all-gather.8
  99.6 148.8 all-gather.10
  250.8 88.2 all-gather.6
